TPU v7x, 32 devices: a whole 2x2x4 slice. The times are simulated.
32 devices in a mesh: survey: 2 (over x), sector: 16 (over z, y, core).
Axes of the slice: x: 2, y: 2, z: 4, core: 2. Of those that a mesh axis runs over, the one named last changes fastest.
Arguments:
- raw_pings: bfloat16 [32, 512, 2, 1024], P('survey', 'sector'), parts along dimension 0, may hold values from -6 to 6
- focus_matrix: bfloat16 [2, 2048, 512], replicated, may hold values from -0.25 to 0.25
- start_angle: int32 [32], P('survey'), parts along dimension 0, may hold values from 0 to 2047
- ping_count: int32 [32], P('survey'), parts along dimension 0, may hold values from 256 to 512, as said below
Outputs:
- coherence: float32 [32, 2048, 1024], P(('survey', 'sector')), parts along dimension 0
- interferogram: bfloat16 [32, 2, 2048, 1024], P(('survey', 'sector')), parts along dimension 0
There are 2 independent parts, one for each index of `survey`. A program takes and returns all parts, laid end to end along the dimension named above; an argument that names none is the same for every part. Nothing has to cross between parts.
Inputs may be any that keep to these rules, and one draw needn't show every extreme that they name: `ping_count`: every value lies between 256 and 512, and at least one sector holds all 512 pings.
All inputs are finite; a program needn't handle non-finite values.
Results may differ from a plain program's by a relative error of at most 0.0057.
Values may be sent and summed in bfloat16 or wider, within the bound.
A program may use at most 192 MiB of HBM per device.

v0:
```python
import jax
import jax.numpy as jnp
from jax import lax
from jax.sharding import PartitionSpec as P

WIN = 9


def shifted(block, axis, distance):
    devices = range(lax.axis_size(axis))
    route = [((i - distance) % len(devices), i) for i in devices]
    return lax.ppermute(block, axis, route)


def focus_sector(raw, angle_step, valid_pings, stacked):
    pings_here = raw.shape[0]
    ranges_here = raw.shape[2]
    columns_count = stacked.shape[0] // 2
    ping_mask = (jnp.arange(pings_here, dtype=jnp.int32) < valid_pings).astype(jnp.bfloat16)
    masked = raw * ping_mask[:, None, None]
    product = jnp.dot(
        stacked, masked.reshape(pings_here, 2 * ranges_here), preferred_element_type=jnp.float32
    )
    product = product.reshape(2, columns_count, 2, ranges_here)
    real_part = product[0, :, 0] - product[1, :, 1]
    imag_part = product[0, :, 1] + product[1, :, 0]
    columns = jnp.arange(columns_count, dtype=jnp.int32)
    turn_index = angle_step * columns % columns_count
    phase_turn = 2.0 * jnp.pi / columns_count * turn_index.astype(jnp.float32)
    cosine = jnp.cos(phase_turn)[:, None]
    sine_part = jnp.sin(phase_turn)[:, None]
    mean_power = jnp.mean(real_part * real_part + imag_part * imag_part, axis=0)
    inverse_rms = lax.rsqrt(mean_power + 1e-06)
    turned_real = (real_part * cosine + imag_part * sine_part) * inverse_rms
    turned_imag = (imag_part * cosine - real_part * sine_part) * inverse_rms
    return jnp.stack([turned_real, turned_imag], axis=1).astype(jnp.bfloat16)


def window_sum(field, axis, span):
    half_span = span // 2
    length_axis = field.shape[axis]
    widths = [(0, 0)] * field.ndim
    widths[axis] = (half_span, half_span)
    padded = jnp.pad(field, widths)
    total = lax.slice_in_dim(padded, 0, length_axis, axis=axis)
    for offset in range(1, span):
        total = total + lax.slice_in_dim(padded, offset, offset + length_axis, axis=axis)
    return total


def compare(own_image, other_image, span):
    f_real = own_image[:, 0].astype(jnp.float32)
    f_imag = own_image[:, 1].astype(jnp.float32)
    g_real = other_image[:, 0].astype(jnp.float32)
    g_imag = other_image[:, 1].astype(jnp.float32)
    fields = jnp.stack(
        [
            f_real * g_real + f_imag * g_imag,
            f_imag * g_real - f_real * g_imag,
            f_real * f_real + f_imag * f_imag,
            g_real * g_real + g_imag * g_imag,
        ],
        axis=0,
    )
    looked = window_sum(window_sum(fields, 1, span), 2, span)
    magnitude = jnp.sqrt(looked[0] * looked[0] + looked[1] * looked[1])
    energy = jnp.sqrt(looked[2] * looked[3] + 1e-06)
    coherence = magnitude / energy
    interferogram = (looked[0:2] / float(span * span)).astype(jnp.bfloat16)
    return (coherence, interferogram)


def body(raw_pings, focus_matrix, start_angle, ping_count):
    stacked = focus_matrix.reshape(2 * focus_matrix.shape[1], focus_matrix.shape[2])
    position = lax.axis_index("sector")

    def prepare(pieces, sector):
        return focus_sector(pieces[0], start_angle[sector], ping_count[sector], stacked)[None]

    own_image = (lambda pieces: prepare(pieces, position))(
        lax.all_to_all(raw_pings, "sector", split_axis=0, concat_axis=1, tiled=True)
    )
    other_image = shifted(own_image, "sector", -1)
    coherence, interferogram = compare(own_image[0], other_image[0], WIN)
    return (coherence[None], interferogram[None])


def solution(mesh):
    return jax.shard_map(
        body,
        mesh=mesh,
        in_specs=(P("survey", "sector", None, None), P(), P("survey"), P("survey")),
        out_specs=(P(("survey", "sector"), None, None), P(("survey", "sector"), None, None, None)),
        check_vma=False,
    )
```

profile of v0, /device:TPU:0, one launch (start us, length us, event | category | flops | bytes accessed | tf_op | source)
XLA Modules:
  0.0 722.9 jit_solution(4973740520128592052)
XLA Ops:
  0.6 7.4 %all-to-all-start = ((bf16[16,32,2,1024]{3,2,1,0:T(2,128)(2,1)}), bf16[16,32,2,1024]{3,2,1,0:T(2,128)(2,1)S(1)}, u32[]{:S(2)}, u32[]{:S(2)}) async-start(bf16[16,32,2,1024]{3,2,1,0:T(2,128)(2,1)} %param.4), calls=%async_computation | async-start | bytes 4194304 | tf_op jit(solution)/shard_map/all_to_all | solution.py:81
  8.0 1.2 dynamic_slice.6
  9.3 1.2 dynamic_slice.7
  10.5 0.7 fusion.37
  11.2 0.7 fusion.38
  11.9 37.3 %all-to-all-done = bf16[16,32,2,1024]{3,2,1,0:T(2,128)(2,1)S(1)} async-done(((bf16[16,32,2,1024]{3,2,1,0:T(2,128)(2,1)}), bf16[16,32,2,1024]{3,2,1,0:T(2,128)(2,1)S(1)}, u32[]{:S(2)}, u32[]{:S(2)}) %all-to-all-start) | async-done | bytes 2097184 | tf_op jit(solution)/shard_map/all_to_all | solution.py:81
  49.1 1.9 broadcast_multiply_fusion
  51.0 0.6 copy.14
  51.6 17.5 %convolution_bitcast_fusion = f32[4096,2048]{0,1:T(8,128)} fusion(bf16[512,2048]{1,0:T(8,128)(2,1)S(1)} %bitcast.52, bf16[4096,512]{1,0:T(8,128)(2,1)} %bitcast.53), kind=kOutput, calls=%fused_computation.23 | convolution fusion | flops 8589934592 | bytes 39845888 | tf_op jit(solution)/shard_map/dot_general | solution.py:21
  69.1 42.6 %reshape.411 = f32[2,2048,2,1024]{1,0,3,2:T(2,128)} reshape(f32[4096,2048]{0,1:T(8,128)} %convolution_bitcast_fusion) | data formatting | bytes 67108864 | tf_op jit(solution)/shard_map/reshape | solution.py:24
  111.8 39.8 %fusion.42 = (f32[1,2048,1,1024]{1,0,3,2:T(1,128)}, f32[1,2048,1,1024]{1,0,3,2:T(1,128)}, f32[1,2048,1,1024]{1,0,3,2:T(1,128)}, f32[1,2048,1,1024]{1,0,3,2:T(1,128)}) fusion(f32[2,2048,2,1024]{1,0,3,2:T(2,128)} %reshape.411), kind=kLoop, calls=%fused_computation.80 | loop fusion | bytes 67108864 | tf_op jit(solution)/shard_map/slice | solution.py:25
  151.6 20.7 %copy.10 = f32[1,2048,1,1024]{3,1,2,0:T(8,128)} copy(f32[1,2048,1,1024]{1,0,3,2:T(1,128)} %get-tuple-element.10) | data formatting | bytes 16777216
  172.4 20.7 %copy.11 = f32[1,2048,1,1024]{3,1,2,0:T(8,128)} copy(f32[1,2048,1,1024]{1,0,3,2:T(1,128)} %get-tuple-element.8) | data formatting | bytes 16777216
  193.0 20.5 %copy.12 = f32[1,2048,1,1024]{3,1,2,0:T(8,128)} copy(f32[1,2048,1,1024]{1,0,3,2:T(1,128)} %get-tuple-element.9) | data formatting | bytes 16777216
  213.6 20.5 %copy.13 = f32[1,2048,1,1024]{3,1,2,0:T(8,128)} copy(f32[1,2048,1,1024]{1,0,3,2:T(1,128)} %get-tuple-element.11) | data formatting | bytes 16777216
  234.1 19.2 %add_reduce_fusion = (f32[1024]{0:T(1024)S(1)}, f32[1,2048,1,1024]{3,1,2,0:T(8,128)}, f32[1,2048,1,1024]{3,1,2,0:T(8,128)}) fusion(f32[1,2048,1,1024]{3,1,2,0:T(8,128)} %copy.12, f32[1,2048,1,1024]{3,1,2,0:T(8,128)} %copy.13, f32[1,2048,1,1024]{3,1,2,0:T(8,128)} %copy.10, f32[1,2048,1,1024]{3,1,2,0:T(8,128)} %copy.11), kind=kLoop, calls=%fused_computation.64 | loop fusion | flops 12581888 | bytes 50335744 | tf_op jit(solution)/shard_map/reduce_sum | solution.py:32
  253.4 8.6 %multiply_convert_fusion.1 = (bf16[1,2048,1,1024]{3,1,2,0:T(8,128)(2,1)S(1)}, bf16[1,2048,1,1024]{3,1,2,0:T(8,128)(2,1)}) fusion(f32[1,2048,1,1024]{3,1,2,0:T(8,128)} %get-tuple-element.6, f32[1,2048,1,1024]{3,1,2,0:T(8,128)} %get-tuple-element.7, f32[1024]{0:T(1024)S(1)} %add_rsqrt_fusion, f32[2048]{0:T(1024)S(1)} %get-tuple-element.17, ...), kind=kLoop, calls=%fused_computation.63 | loop fusion | flops 20971520 | bytes 25186304 | tf_op jit(solution)/shard_map/convert
  262.0 6.2 pad_maximum_fusion.1
  268.1 9.7 %collective-permute-start = (bf16[1,2048,2,1024]{3,1,2,0:T(8,128)(2,1)}, bf16[1,2048,2,1024]{3,1,2,0:T(8,128)(2,1)S(1)}, u32[]{:S(2)}, u32[]{:S(2)}) collective-permute-start(bf16[1,2048,2,1024]{3,1,2,0:T(8,128)(2,1)} %pad_maximum_fusion.1), channel_id=1, source_target_pairs={{1,0},{2,1},{3,2},{4,3},{5,4},{6,5},{7,6},{8,7},{9,8},{10,9},{11,1... | collective-permute-start | bytes 25165832 | tf_op jit(solution)/shard_map/ppermute | solution.py:12
  277.9 91.3 %collective-permute-done = bf16[1,2048,2,1024]{3,1,2,0:T(8,128)(2,1)S(1)} collective-permute-done((bf16[1,2048,2,1024]{3,1,2,0:T(8,128)(2,1)}, bf16[1,2048,2,1024]{3,1,2,0:T(8,128)(2,1)S(1)}, u32[]{:S(2)}, u32[]{:S(2)}) %collective-permute-start) | collective-permute-done | bytes 8388640 | tf_op jit(solution)/shard_map/ppermute | solution.py:12
  369.2 13.3 %fusion.14 = (f32[1,2048,1024]{2,1,0:T(8,128)}, bf16[2048,1,1024]{2,0,1:T(8,128)(2,1)S(1)}, bf16[2048,1,1024]{2,0,1:T(8,128)(2,1)}) fusion(bf16[2048,2,1024]{2,0,1:T(8,128)(2,1)S(1)} %bitcast.49, f32[1024]{0:T(1024)S(1)} %add_rsqrt_fusion, f32[2048]{0:T(1024)S(1)} %get-tuple-element.17, f32[1,2048,1,1024]{3,1,2,0:T(8,128)} %get-tuple-element.7, ...), kind=kLoop, calls=%fused_computation.37 | loop fusion | flops 35651584 | bytes 41963520 | tf_op jit(solution)/shard_map/add | solution.py:58
  382.5 11.1 %fusion.18 = (f32[1,2048,1024]{2,1,0:T(8,128)}, f32[1,2048,1024]{2,1,0:T(8,128)}, f32[1,2048,1024]{2,1,0:T(8,128)}) fusion(bf16[2048,1,1024]{2,0,1:T(8,128)(2,1)S(1)} %get-tuple-element.3, bf16[2048,1,1024]{2,0,1:T(8,128)(2,1)} %get-tuple-element.4, bf16[2048,2,1024]{2,0,1:T(8,128)(2,1)S(1)} %bitcast.50), kind=kLoop, calls=%fused_computation.41 | loop fusion | flops 27262976 | bytes 41943040 | tf_op jit(solution)/shard_map/sub | solution.py:59
  393.6 23.4 %pad_maximum_fusion = f32[4,2048,1024]{2,1,0:T(8,128)} fusion(f32[1,2048,1024]{2,1,0:T(8,128)} %get-tuple-element.15, f32[1,2048,1024]{2,1,0:T(8,128)} %get-tuple-element.16, f32[1,2048,1024]{2,1,0:T(8,128)} %get-tuple-element.14, f32[1,2048,1024]{2,1,0:T(8,128)} %get-tuple-element.2), kind=kLoop, calls=%fused_computation.16 | loop fusion | flops 25165824 | bytes 67108864 | tf_op jit(solution)/shard_map/stack | solution.py:56
  417.0 131.8 %slice_add_fusion = f32[4,2048,1024]{2,1,0:T(8,128)} fusion(f32[4,2048,1024]{2,1,0:T(8,128)} %pad_maximum_fusion), kind=kLoop, calls=%fused_computation.17 | loop fusion | flops 67108864 | bytes 67108864 | tf_op jit(solution)/shard_map/add | solution.py:47
  548.8 147.7 %fusion.7 = f32[4,2048,1024]{2,1,0:T(8,128)} fusion(f32[4,2048,1024]{2,1,0:T(8,128)} %slice_add_fusion), kind=kLoop, calls=%fused_computation.15 | loop fusion | flops 67108864 | bytes 67108864 | tf_op jit(solution)/shard_map/add | solution.py:47
  696.5 9.6 %fusion.19 = bf16[1,2,2048,1024]{3,2,1,0:T(8,128)(2,1)} fusion(f32[4,2048,1024]{2,1,0:T(8,128)} %fusion.7), kind=kLoop, calls=%fused_computation.42 | loop fusion | flops 8388608 | bytes 25165824 | tf_op jit(solution)/shard_map/broadcast_in_dim | solution.py:85
  706.1 16.7 %fusion.22 = f32[1,2048,1024]{2,1,0:T(8,128)} fusion(f32[4,2048,1024]{2,1,0:T(8,128)} %fusion.7), kind=kLoop, calls=%fused_computation.46 | loop fusion | flops 12582912 | bytes 41943040 | tf_op jit(solution)/shard_map/div | solution.py:68
  (1 shorter events, 0.0 us)
Async XLA Ops:
  0.6 48.5 %all-to-all-start = ((bf16[16,32,2,1024]{3,2,1,0:T(2,128)(2,1)}), bf16[16,32,2,1024]{3,2,1,0:T(2,128)(2,1)S(1)}, u32[]{:S(2)}, u32[]{:S(2)}) async-start(bf16[16,32,2,1024]{3,2,1,0:T(2,128)(2,1)} %param.4), calls=%async_computation | async-start | bytes 4194304 | tf_op jit(solution)/shard_map/all_to_all | solution.py:81
  268.1 101.0 %collective-permute-start = (bf16[1,2048,2,1024]{3,1,2,0:T(8,128)(2,1)}, bf16[1,2048,2,1024]{3,1,2,0:T(8,128)(2,1)S(1)}, u32[]{:S(2)}, u32[]{:S(2)}) collective-permute-start(bf16[1,2048,2,1024]{3,1,2,0:T(8,128)(2,1)} %pad_maximum_fusion.1), channel_id=1, source_target_pairs={{1,0},{2,1},{3,2},{4,3},{5,4},{6,5},{7,6},{8,7},{9,8},{10,9},{11,1... | collective-permute-start | bytes 25165832 | tf_op jit(solution)/shard_map/ppermute | solution.py:12
where the time goes:
time: 726 us; the launch traced here: 723 us
  other arithmetic  391 us (54%)
  local copies, waits for them, and re-layouts  168 us (23%)
  waiting for transfers between devices  129 us (18%)
  matrix products  17.5 us (2%)
  starting transfers between devices  17.1 us (2%)
    add x2, other arithmetic, window_sum(): total + lax.slice_in_dim(padded, offset, offset + length_axis, axis=axis)  280 us
    ppermute x1, waiting for transfers between devices, shifted(): return lax.ppermute(block, axis, route)  91.3 us
    unnamed x5, local copies, waits for them, and re-layouts  83.1 us
    reshape x1, local copies, waits for them, and re-layouts, focus_sector(): product = product.reshape(2, columns_count, 2, ranges_here)  42.6 us
    slice x1, local copies, waits for them, and re-layouts, focus_sector(): real_part = product[0, :, 0] - product[1, :, 1]  39.8 us
    all_to_all x1, waiting for transfers between devices, body(): lax.all_to_all(raw_pings, 'sector', split_axis=0, concat_axis=1, tiled=True)  37.3 us
    another operation x1, other arithmetic, compare(): jnp.stack([f_real * g_real + f_imag * g_imag, f_imag * g_real - f_real *...  23.4 us
    reduce_sum x1, other arithmetic, focus_sector(): mean_power = jnp.mean(real_part * real_part + imag_part * imag_part, axis=0)  19.2 us
  transfers between devices with their start and end apart: 2, of which 2 were waited for; matrix products, arithmetic and copies ran while one was open for 1% of the time, Pallas kernels for 0%

commit v1 on v0

v1 whole, which is shorter than its diff:
```python
import functools

import jax
import jax.numpy as jnp
from jax import lax
from jax.experimental import pallas as pl
from jax.experimental.pallas import tpu as pltpu
from jax.sharding import PartitionSpec as P

WIN = 9
ROWS = 256
HALO = 128
STRIP = 16
CHUNKS = 4


def window_start(tile, size, length):
    return min(max(tile * size - HALO, 0), length - size - 2 * HALO)


def bands(size):
    k = jnp.arange(size + 2 * HALO)[None, :, None]
    n = jnp.arange(size)[None, None, :]
    d = jnp.arange(3)[:, None, None] * HALO
    return (jnp.abs(k - d - n) <= WIN // 2).astype(jnp.bfloat16)


def focus_kernel(tiles, x_ref, h_ref, trig_ref, band_ref, s_ref, turn_ref, raw_ref, power_ref, field_ref):
    step = pl.program_id(0)
    width = s_ref.shape[2]
    length = tiles * ROWS

    @pl.when(step == 0)
    def _():
        power_ref[...] = jnp.zeros_like(power_ref)
        for image in range(2):
            turn_ref[image, :, :width] = -x_ref[image, :, width:]
            turn_ref[image, :, width:] = x_ref[image, :, :width]

    @pl.when(step < tiles)
    def _():
        rows = pl.ds(pl.multiple_of(step * ROWS, ROWS), ROWS)
        for image in range(2):
            product = jnp.dot(h_ref[0], x_ref[image], preferred_element_type=jnp.float32)
            product += jnp.dot(h_ref[1], turn_ref[image], preferred_element_type=jnp.float32)
            raw_ref[image, rows, :] = product
            square = product * product
            square = square[:, :width] + square[:, width:]
            power_ref[image] += jnp.sum(square.reshape(ROWS // 8, 8, width), axis=0)

    @pl.when((step >= tiles) & (step < 2 * tiles))
    def _():
        base = (step - tiles) * ROWS
        inverse = [
            lax.rsqrt(jnp.sum(power_ref[image], axis=0, keepdims=True) * (1.0 / length) + 1e-06)
            for image in range(2)
        ]
        for strip in range(ROWS // STRIP):
            rows = pl.ds(pl.multiple_of(base + strip * STRIP, STRIP), STRIP)
            parts = []
            for image in range(2):
                local = slice(strip * STRIP, (strip + 1) * STRIP)
                cosine = trig_ref[local, 2 * image : 2 * image + 1]
                sine = trig_ref[local, 2 * image + 1 : 2 * image + 2]
                real = raw_ref[image, rows, :width]
                imag = raw_ref[image, rows, width:]
                turned_real = (real * cosine + imag * sine) * inverse[image]
                turned_imag = (imag * cosine - real * sine) * inverse[image]
                parts.append(turned_real.astype(jnp.bfloat16).astype(jnp.float32))
                parts.append(turned_imag.astype(jnp.bfloat16).astype(jnp.float32))
            fr, fi, gr, gi = parts
            field_ref[0, rows, :] = (fr * gr + fi * gi).astype(jnp.bfloat16)
            field_ref[1, rows, :] = (fi * gr - fr * gi).astype(jnp.bfloat16)
            field_ref[2, rows, :] = (fr * fr + fi * fi).astype(jnp.bfloat16)
            field_ref[3, rows, :] = (gr * gr + gi * gi).astype(jnp.bfloat16)

    @pl.when(step > tiles)
    def _():
        tile = step - tiles - 1
        start = jnp.clip(tile * ROWS - HALO, 0, length - ROWS - 2 * HALO)
        rows = pl.ds(pl.multiple_of(start, HALO), ROWS + 2 * HALO)
        which = jnp.where(tile == 0, 0, jnp.where(tile == tiles - 1, 2, 1))
        band = band_ref[which]
        for field in range(4):
            total = jnp.dot(band, field_ref[field, rows, :], preferred_element_type=jnp.float32)
            s_ref[field] = total.astype(jnp.bfloat16)


def focus(pings, matrix, trig):
    _, depth, double = pings.shape
    width = double // 2
    length = matrix.shape[1]
    tiles = length // ROWS
    band = jnp.swapaxes(bands(ROWS), 1, 2)
    return pl.pallas_call(
        functools.partial(focus_kernel, tiles),
        grid=(2 * tiles + 1,),
        in_specs=[
            pl.BlockSpec((2, depth, double), lambda t: (0, 0, 0)),
            pl.BlockSpec((2, ROWS, depth), lambda t: (0, jnp.minimum(t, tiles - 1), 0)),
            pl.BlockSpec((ROWS, 4), lambda t: (jnp.clip(t - tiles, 0, tiles - 1), 0)),
            pl.BlockSpec(band.shape, lambda t: (0, 0, 0)),
        ],
        out_specs=pl.BlockSpec((4, ROWS, width), lambda t: (0, jnp.clip(t - tiles - 1, 0, tiles - 1), 0)),
        out_shape=jax.ShapeDtypeStruct((4, length, width), jnp.bfloat16),
        scratch_shapes=[
            pltpu.VMEM((2, depth, double), jnp.bfloat16),
            pltpu.VMEM((2, length, double), jnp.float32),
            pltpu.VMEM((2, 8, width), jnp.float32),
            pltpu.VMEM((4, length, width), jnp.bfloat16),
        ],
        compiler_params=pltpu.CompilerParams(
            dimension_semantics=("arbitrary",), vmem_limit_bytes=32 * 2**20
        ),
        cost_estimate=pl.CostEstimate(
            flops=16 * length * depth * width + 16 * length * width * ROWS,
            bytes_accessed=4 * length * depth + 8 * length * width,
            transcendentals=0,
        ),
        name="focus",
    )(pings, matrix, trig, band)


def compare_kernel(chunks, band_ref, *refs):
    s_refs, (coherence_ref, inter_ref) = refs[:chunks], refs[chunks:]
    width = s_refs[0].shape[2]
    rows = s_refs[0].shape[1]
    for part in range(chunks):
        first = window_start(part, width, width * chunks)
        band = band_ref[(part * width - first) // HALO]
        sums = []
        for field in range(4):
            pieces = []
            for chunk in range(chunks):
                low = max(first, chunk * width) - chunk * width
                high = min(first + width + 2 * HALO, (chunk + 1) * width) - chunk * width
                if high > low:
                    pieces.append(s_refs[chunk][field, :, low:high])
            block = jnp.concatenate(pieces, axis=1)
            sums.append(jnp.dot(block, band, preferred_element_type=jnp.float32))
        real, imag, own, other = sums
        lanes = slice(part * width, (part + 1) * width)
        magnitude = jnp.sqrt(real * real + imag * imag)
        coherence_ref[0, :, lanes] = magnitude * lax.rsqrt(own * other + 1e-06)
        inter_ref[0, 0, :, lanes] = (real * (1.0 / (WIN * WIN))).astype(jnp.bfloat16)
        inter_ref[0, 1, :, lanes] = (imag * (1.0 / (WIN * WIN))).astype(jnp.bfloat16)


def compare(parts):
    chunks = len(parts)
    _, length, width = parts[0].shape
    ranges = width * chunks
    band = bands(width)
    return pl.pallas_call(
        functools.partial(compare_kernel, chunks),
        grid=(length // ROWS,),
        in_specs=[pl.BlockSpec(band.shape, lambda t: (0, 0, 0))]
        + [pl.BlockSpec((4, ROWS, width), lambda t: (0, t, 0))] * chunks,
        out_specs=[
            pl.BlockSpec((1, ROWS, ranges), lambda t: (0, t, 0)),
            pl.BlockSpec((1, 2, ROWS, ranges), lambda t: (0, 0, t, 0)),
        ],
        out_shape=[
            jax.ShapeDtypeStruct((1, length, ranges), jnp.float32),
            jax.ShapeDtypeStruct((1, 2, length, ranges), jnp.bfloat16),
        ],
        compiler_params=pltpu.CompilerParams(
            dimension_semantics=("arbitrary",), vmem_limit_bytes=32 * 2**20
        ),
        cost_estimate=pl.CostEstimate(
            flops=16 * length * ranges * width, bytes_accessed=16 * length * ranges, transcendentals=0
        ),
        name="compare",
    )(band, *parts)


def turn_table(angle, length):
    index = angle * jnp.arange(length, dtype=jnp.int32) % length
    phase = 2.0 * jnp.pi / length * index.astype(jnp.float32)
    return [jnp.cos(phase), jnp.sin(phase)]


def body(raw_pings, focus_matrix, start_angle, ping_count):
    sectors = lax.axis_size("sector")
    length, depth = focus_matrix.shape[1:]
    position = lax.axis_index("sector")
    following = lax.rem(position + 1, sectors)
    route = [((i + 1) % sectors, i) for i in range(sectors)]
    trig = jnp.stack(
        turn_table(start_angle[position], length) + turn_table(start_angle[following], length), axis=1
    )
    ping = jnp.arange(depth, dtype=jnp.int32)[:, None]

    def masked(block, sector):
        flat = block.reshape(depth, -1)
        return jnp.where(ping < ping_count[sector], flat, jnp.zeros_like(flat))

    width = raw_pings.shape[3] // CHUNKS
    parts = []
    for chunk in range(CHUNKS):
        piece = raw_pings[:, :, :, chunk * width : (chunk + 1) * width]
        own = lax.all_to_all(piece, "sector", split_axis=0, concat_axis=1, tiled=True)
        other = lax.ppermute(own, "sector", route)
        pings = jnp.stack([masked(own, position), masked(other, following)])
        parts.append(focus(pings, focus_matrix, trig))
    return tuple(compare(parts))


def solution(mesh):
    return jax.shard_map(
        body,
        mesh=mesh,
        in_specs=(P("survey", "sector", None, None), P(), P("survey"), P("survey")),
        out_specs=(P(("survey", "sector"), None, None), P(("survey", "sector"), None, None, None)),
        check_vma=False,
    )
```

time: 726 us -> 195 us (0.27)
  other arithmetic: 391 us -> 10.7 us
  local copies, waits for them, and re-layouts: 168 us -> 22.9 us
  waiting for transfers between devices: 129 us -> 17.5 us
  Pallas kernels: 0 us -> 68.5 us
  blocking collectives: 0 us -> 40.3 us
  matrix products: 17.5 us -> 0 us
  starting transfers between devices: 17.1 us -> 32.8 us
    add x3 -> x0, other arithmetic: 293 us -> none  [the longest x2 280 us: window_sum(): total + lax.slice_in_dim(padded, offset, offset + length_axis, axis=axis)]
    ppermute x1 -> x4, waiting for transfers between devices: 91.3 us -> 0.01 us  [body(): other = lax.ppermute(own, 'sector', route)]
    unnamed x5 -> x14, local copies, waits for them, and re-layouts: 83.1 us -> 1.98 us
    pallas_call x0 -> x5, Pallas kernels: none -> 68.5 us  [the longest x4 55.8 us: focus(): pl.pallas_call(functools.partial(focus_kernel, tiles), grid=(2 * tiles +...]
    all_to_all x0 -> x2, blocking collectives: none -> 40.3 us  [body(): lax.all_to_all(piece, 'sector', split_axis=0, concat_axis=1, tiled=True)]
    another operation x3 -> x5, other arithmetic: 38.2 us -> 0.43 us  [the longest x4 0.4 us: body(): pings = jnp.stack([masked(own, position), masked(other, following)])]
    slice x1, local copies, waits for them, and re-layouts: 39.8 us -> 4.1 us  [body(): piece = raw_pings[:, :, :, chunk * width:(chunk + 1) * width]]
    reshape x1 -> x8, local copies, waits for them, and re-layouts: 42.6 us -> 15.8 us  [masked(): flat = block.reshape(depth, -1)]
  transfers between devices with their start and end apart: 2 -> 6, of which waited for: 2 -> 2; matrix products, arithmetic and copies ran while one was open for 1% -> 12% of each run, Pallas kernels for 0% -> 0%
where the time goes in v1:
time: 195 us; the launch traced here: 194 us
  Pallas kernels  68.5 us (35%)
  blocking collectives  40.3 us (21%)
  starting transfers between devices  32.8 us (17%)
  local copies, waits for them, and re-layouts  22.9 us (12%)
  waiting for transfers between devices  17.5 us (9%)
  other arithmetic  10.7 us (5%)
    pallas_call x4, Pallas kernels, focus(): pl.pallas_call(functools.partial(focus_kernel, tiles), grid=(2 * tiles +...  55.8 us
    all_to_all x2, blocking collectives, body(): lax.all_to_all(piece, 'sector', split_axis=0, concat_axis=1, tiled=True)  40.3 us
    ppermute x4, starting transfers between devices, body(): other = lax.ppermute(own, 'sector', route)  24.4 us
    all_to_all x2, waiting for transfers between devices, body(): lax.all_to_all(piece, 'sector', split_axis=0, concat_axis=1, tiled=True)  17.5 us
    reshape x8, local copies, waits for them, and re-layouts, masked(): flat = block.reshape(depth, -1)  15.8 us
    pallas_call x1, Pallas kernels, compare(): pl.pallas_call(functools.partial(compare_kernel, chunks), grid=(length //...  12.8 us
    all_to_all x2, starting transfers between devices, body(): lax.all_to_all(piece, 'sector', split_axis=0, concat_axis=1, tiled=True)  8.49 us
    select_n x2, other arithmetic, masked(): return jnp.where(ping < ping_count[sector], flat, jnp.zeros_like(flat))  4.53 us
  transfers between devices with their start and end apart: 6, of which 2 were waited for; matrix products, arithmetic and copies ran while one was open for 12% of the time, Pallas kernels for 0%

profile of v1, /device:TPU:0, one launch (start us, length us, event | category | flops | bytes accessed | tf_op | source)
XLA Modules:
  0.0 193.7 jit_solution(12014572409243715730)
XLA Ops:
  0.6 4.1 %fusion.12 = (bf16[16,32,2,256]{3,2,1,0:T(2,128)(2,1)}, bf16[16,32,2,256]{3,2,1,0:T(2,128)(2,1)S(1)}, bf16[16,32,2,256]{3,2,1,0:T(2,128)(2,1)S(1)}, bf16[16,32,2,256]{3,2,1,0:T(2,128)(2,1)}) fusion(bf16[16,32,2,1024]{3,2,1,0:T(2,128)(2,1)} %param.4), kind=kLoop, calls=%fused_computation.37 | loop fusion | bytes 4194304 | tf_op jit(solution)/shard_map/slice | solution.py:201
  4.7 21.9 %all_to_all.48 = bf16[16,32,2,256]{3,2,1,0:T(2,128)(2,1)} all-to-all(bf16[16,32,2,256]{3,2,1,0:T(2,128)(2,1)S(1)} %get-tuple-element.3), channel_id=1, replica_groups=mesh['survey'=2,'sector'=16] {'sector'}, dimensions={0} | all-to-all | bytes 1048576 | tf_op jit(solution)/shard_map/all_to_all | solution.py:202
  26.6 18.5 %all_to_all.49 = bf16[16,32,2,256]{3,2,1,0:T(2,128)(2,1)} all-to-all(bf16[16,32,2,256]{3,2,1,0:T(2,128)(2,1)S(1)} %get-tuple-element.4), channel_id=1, replica_groups=mesh['survey'=2,'sector'=16] {'sector'}, dimensions={0} | all-to-all | bytes 1048576 | tf_op jit(solution)/shard_map/all_to_all | solution.py:202
  45.1 4.2 %all-to-all-start.2 = ((bf16[16,32,2,256]{3,2,1,0:T(2,128)(2,1)}), bf16[16,32,2,256]{3,2,1,0:T(2,128)(2,1)}, u32[]{:S(2)}, u32[]{:S(2)}) async-start(bf16[16,32,2,256]{3,2,1,0:T(2,128)(2,1)} %get-tuple-element.5), calls=%async_computation.2 | async-start | bytes 1048576 | tf_op jit(solution)/shard_map/all_to_all | solution.py:202
  49.4 0.7 fusion.13
  50.0 0.9 fusion.10
  50.9 0.9 fusion.11
  51.8 0.9 fusion.8
  52.7 0.9 fusion.9
  53.7 10.1 %all-to-all-done.2 = bf16[16,32,2,256]{3,2,1,0:T(2,128)(2,1)} async-done(((bf16[16,32,2,256]{3,2,1,0:T(2,128)(2,1)}), bf16[16,32,2,256]{3,2,1,0:T(2,128)(2,1)}, u32[]{:S(2)}, u32[]{:S(2)}) %all-to-all-start.2) | async-done | bytes 524320 | tf_op jit(solution)/shard_map/all_to_all | solution.py:202
  63.8 4.2 %all-to-all-start.3 = ((bf16[16,32,2,256]{3,2,1,0:T(2,128)(2,1)}), bf16[16,32,2,256]{3,2,1,0:T(2,128)(2,1)}, u32[]{:S(2)}, u32[]{:S(2)}) async-start(bf16[16,32,2,256]{3,2,1,0:T(2,128)(2,1)} %get-tuple-element.2), calls=%async_computation.3 | async-start | bytes 1048576 | tf_op jit(solution)/shard_map/all_to_all | solution.py:202
  68.1 0.4 copy.6.trig_ref
  68.5 0.6 iota_compare_fusion
  69.1 0.7 iota_compare_fusion.1
  69.7 0.1 iota_subtract_fusion
  69.8 0.4 fusion.1.band_ref
  70.2 4.3 %collective-permute-start.2 = (bf16[1,512,2,256]{3,2,1,0:T(2,128)(2,1)}, bf16[1,512,2,256]{3,2,1,0:T(2,128)(2,1)}, u32[]{:S(2)}, u32[]{:S(2)}) collective-permute-start(bf16[1,512,2,256]{3,2,1,0:T(2,128)(2,1)} %bitcast.6), channel_id=1, source_target_pairs={{1,0},{2,1},{3,2},{4,3},{5,4},{6,5},{7,6},{8,7},{9,8},{10,9},{11,1... | collective-permute-start | bytes 1572872 | tf_op jit(solution)/shard_map/ppermute | solution.py:203
  74.5 0.4 collective-permute-start
  74.9 0.3 collective-permute-start.1
  75.2 7.4 %all-to-all-done.3 = bf16[16,32,2,256]{3,2,1,0:T(2,128)(2,1)} async-done(((bf16[16,32,2,256]{3,2,1,0:T(2,128)(2,1)}), bf16[16,32,2,256]{3,2,1,0:T(2,128)(2,1)}, u32[]{:S(2)}, u32[]{:S(2)}) %all-to-all-start.3) | async-done | bytes 524320 | tf_op jit(solution)/shard_map/all_to_all | solution.py:202
  82.6 19.4 %collective-permute-start.3 = (bf16[1,512,2,256]{3,2,1,0:T(2,128)(2,1)}, bf16[1,512,2,256]{3,2,1,0:T(2,128)(2,1)}, u32[]{:S(2)}, u32[]{:S(2)}) collective-permute-start(bf16[1,512,2,256]{3,2,1,0:T(2,128)(2,1)} %bitcast.7), channel_id=1, source_target_pairs={{1,0},{2,1},{3,2},{4,3},{5,4},{6,5},{7,6},{8,7},{9,8},{10,9},{11,1... | collective-permute-start | bytes 1572872 | tf_op jit(solution)/shard_map/ppermute | solution.py:203
  101.9 0.4 fusion.band_ref
  102.3 1.4 reshape.429
  103.7 2.2 %reshape.425 = bf16[1,512,512]{2,1,0:T(8,128)(2,1)} reshape(bf16[16,32,2,256]{3,2,1,0:T(2,128)(2,1)} %all_to_all.49) | data formatting | bytes 1048576 | tf_op jit(solution)/shard_map/reshape | solution.py:195
  105.9 2.2 %reshape.427 = bf16[1,512,512]{2,1,0:T(8,128)(2,1)} reshape(bf16[16,32,2,256]{3,2,1,0:T(2,128)(2,1)} %all_to_all.48) | data formatting | bytes 1048576 | tf_op jit(solution)/shard_map/reshape | solution.py:195
  108.1 2.2 %reshape.431 = bf16[1,512,512]{2,1,0:T(8,128)(2,1)} reshape(bf16[16,32,2,256]{3,2,1,0:T(2,128)(2,1)} %all-to-all-done.3) | data formatting | bytes 1048576 | tf_op jit(solution)/shard_map/reshape | solution.py:195
  110.2 2.9 %broadcast_select_fusion.4 = (bf16[1,512,512]{2,1,0:T(8,128)(2,1)}, bf16[1,512,512]{2,1,0:T(8,128)(2,1)}, bf16[1,512,512]{2,1,0:T(8,128)(2,1)}, bf16[1,512,512]{2,1,0:T(8,128)(2,1)}) fusion(bf16[1,512,512]{2,1,0:T(8,128)(2,1)} %reshape.431, pred[512]{0:T(512)(128)(4,1)S(1)} %iota_compare_fusion.1, bf16[1,512,512]{2,1,0:T(8,128)(2,1)} %reshape.427, ...), kind=kLoop, calls=%fused_computation.12 | loop fusion | flops 1048576 | bytes 4194816 | tf_op jit(solution)/shard_map/jit(_where)/select_n | solution.py:196
  113.1 0.0 collective-permute-done.2
  113.1 1.4 reshape.430
  114.5 0.0 collective-permute-done
  114.5 2.2 %reshape.426 = bf16[1,512,512]{2,1,0:T(8,128)(2,1)} reshape(bf16[1,512,2,256]{3,2,1,0:T(2,128)(2,1)} %collective-permute-done) | data formatting | bytes 1048576 | tf_op jit(solution)/shard_map/reshape | solution.py:195
  116.7 0.0 collective-permute-done.1
  116.7 2.2 %reshape.428 = bf16[1,512,512]{2,1,0:T(8,128)(2,1)} reshape(bf16[1,512,2,256]{3,2,1,0:T(2,128)(2,1)} %collective-permute-done.1) | data formatting | bytes 1048576 | tf_op jit(solution)/shard_map/reshape | solution.py:195
  118.8 0.0 collective-permute-done.3
  118.8 2.2 %reshape.432 = bf16[1,512,512]{2,1,0:T(8,128)(2,1)} reshape(bf16[1,512,2,256]{3,2,1,0:T(2,128)(2,1)} %collective-permute-done.3) | data formatting | bytes 1048576 | tf_op jit(solution)/shard_map/reshape | solution.py:195
  121.0 1.7 broadcast_select_fusion
  122.7 0.0 copy-start
  122.7 0.1 pad_maximum_fusion.2.x_ref
  122.8 0.0 copy-done.3
  122.8 0.1 pad_maximum_fusion.x_ref
  122.9 2.0 %copy-done = bf16[2,2048,512]{2,1,0:T(8,128)(2,1)S(1)} copy-done((bf16[2,2048,512]{2,1,0:T(8,128)(2,1)S(1)}, bf16[2,2048,512]{2,1,0:T(8,128)(2,1)}, u32[]{:S(2)}) %copy-start) | copy-done | bytes 4194328
  124.9 13.9 %focus.4.refs_0_ = bf16[4,2048,256]{2,1,0:T(8,128)(2,1)S(1)} custom-call(bf16[2,512,512]{2,1,0:T(8,128)(2,1)S(1)} %pad_maximum_fusion.x_ref, bf16[2,2048,512]{2,1,0:T(8,128)(2,1)S(1)} %copy-done, f32[2048,4]{1,0:T(8,128)S(1)} %copy.6.trig_ref, bf16[3,256,512]{2,1,0:T(8,128)(2,1)S(1)} %fusion.1.band_ref), custom_call_target="tpu_custom_call" | custom-call | flops 6442450944 | bytes 8388608 | tf_op jit(solution)/shard_map/focus/pallas_call | solution.py:95
  138.8 13.9 %focus.6.refs_2_ = bf16[4,2048,256]{2,1,0:T(8,128)(2,1)S(1)} custom-call(bf16[2,512,512]{2,1,0:T(8,128)(2,1)S(1)} %pad_maximum_fusion.2.x_ref, bf16[2,2048,512]{2,1,0:T(8,128)(2,1)S(1)} %copy-done, f32[2048,4]{1,0:T(8,128)S(1)} %copy.6.trig_ref, bf16[3,256,512]{2,1,0:T(8,128)(2,1)S(1)} %fusion.1.band_ref), custom_call_target="tpu_custom_call" | custom-call | flops 6442450944 | bytes 8388608 | tf_op jit(solution)/shard_map/focus/pallas_call | solution.py:95
  152.8 0.1 pad_maximum_fusion.1.x_ref
  152.9 13.9 %focus.5.refs_1_ = bf16[4,2048,256]{2,1,0:T(8,128)(2,1)S(1)} custom-call(bf16[2,512,512]{2,1,0:T(8,128)(2,1)S(1)} %pad_maximum_fusion.1.x_ref, bf16[2,2048,512]{2,1,0:T(8,128)(2,1)S(1)} %copy-done, f32[2048,4]{1,0:T(8,128)S(1)} %copy.6.trig_ref, bf16[3,256,512]{2,1,0:T(8,128)(2,1)S(1)} %fusion.1.band_ref), custom_call_target="tpu_custom_call" | custom-call | flops 6442450944 | bytes 8388608 | tf_op jit(solution)/shard_map/focus/pallas_call | solution.py:95
  166.9 0.1 pad_maximum_fusion.3.x_ref
  167.0 13.9 %focus.7.refs_3_ = bf16[4,2048,256]{2,1,0:T(8,128)(2,1)S(1)} custom-call(bf16[2,512,512]{2,1,0:T(8,128)(2,1)S(1)} %pad_maximum_fusion.3.x_ref, bf16[2,2048,512]{2,1,0:T(8,128)(2,1)S(1)} %copy-done, f32[2048,4]{1,0:T(8,128)S(1)} %copy.6.trig_ref, bf16[3,256,512]{2,1,0:T(8,128)(2,1)S(1)} %fusion.1.band_ref), custom_call_target="tpu_custom_call" | custom-call | flops 6442450944 | bytes 8388608 | tf_op jit(solution)/shard_map/focus/pallas_call | solution.py:95
  180.9 12.8 %compare.22 = (f32[1,2048,1024]{2,1,0:T(8,128)}, bf16[1,2,2048,1024]{3,2,1,0:T(8,128)(2,1)}) custom-call(bf16[3,512,256]{2,1,0:T(8,128)(2,1)S(1)} %fusion.band_ref, bf16[4,2048,256]{2,1,0:T(8,128)(2,1)S(1)} %focus.4.refs_0_, bf16[4,2048,256]{2,1,0:T(8,128)(2,1)S(1)} %focus.5.refs_1_, bf16[4,2048,256]{2,1,0:T(8,128)(2,1)S(1)} %focus.6.refs_2_, ...), custom_call_target="tpu_custom_call" | custom-call | flops 8589934592 | bytes 33554432 | tf_op jit(solution)/shard_map/compare/pallas_call | solution.py:154
  (13 shorter events, 0.1 us)
Async XLA Ops:
  4.7 44.6 %copy-start.5 = (s32[16]{0:T(128)S(1)}, s32[16]{0:T(128)}, u32[]{:S(2)}) copy-start(s32[16]{0:T(128)} %param.6) | copy-start | bytes 196
  4.7 44.6 %copy-start.6 = (s32[16]{0:T(128)S(1)}, s32[16]{0:T(128)}, u32[]{:S(2)}) copy-start(s32[16]{0:T(128)} %param.7) | copy-start | bytes 196
  45.1 18.7 %all-to-all-start.2 = ((bf16[16,32,2,256]{3,2,1,0:T(2,128)(2,1)}), bf16[16,32,2,256]{3,2,1,0:T(2,128)(2,1)}, u32[]{:S(2)}, u32[]{:S(2)}) async-start(bf16[16,32,2,256]{3,2,1,0:T(2,128)(2,1)} %get-tuple-element.5), calls=%async_computation.2 | async-start | bytes 1048576 | tf_op jit(solution)/shard_map/all_to_all | solution.py:202
  63.8 18.8 %all-to-all-start.3 = ((bf16[16,32,2,256]{3,2,1,0:T(2,128)(2,1)}), bf16[16,32,2,256]{3,2,1,0:T(2,128)(2,1)}, u32[]{:S(2)}, u32[]{:S(2)}) async-start(bf16[16,32,2,256]{3,2,1,0:T(2,128)(2,1)} %get-tuple-element.2), calls=%async_computation.3 | async-start | bytes 1048576 | tf_op jit(solution)/shard_map/all_to_all | solution.py:202
  70.2 42.9 %collective-permute-start.2 = (bf16[1,512,2,256]{3,2,1,0:T(2,128)(2,1)}, bf16[1,512,2,256]{3,2,1,0:T(2,128)(2,1)}, u32[]{:S(2)}, u32[]{:S(2)}) collective-permute-start(bf16[1,512,2,256]{3,2,1,0:T(2,128)(2,1)} %bitcast.6), channel_id=1, source_target_pairs={{1,0},{2,1},{3,2},{4,3},{5,4},{6,5},{7,6},{8,7},{9,8},{10,9},{11,1... | collective-permute-start | bytes 1572872 | tf_op jit(solution)/shard_map/ppermute | solution.py:203
  74.5 39.9 %collective-permute-start = (bf16[1,512,2,256]{3,2,1,0:T(2,128)(2,1)}, bf16[1,512,2,256]{3,2,1,0:T(2,128)(2,1)}, u32[]{:S(2)}, u32[]{:S(2)}) collective-permute-start(bf16[1,512,2,256]{3,2,1,0:T(2,128)(2,1)} %bitcast.2), channel_id=1, source_target_pairs={{1,0},{2,1},{3,2},{4,3},{5,4},{6,5},{7,6},{8,7},{9,8},{10,9},{11,1... | collective-permute-start | bytes 1572872 | tf_op jit(solution)/shard_map/ppermute | solution.py:203
  74.9 41.8 %collective-permute-start.1 = (bf16[1,512,2,256]{3,2,1,0:T(2,128)(2,1)}, bf16[1,512,2,256]{3,2,1,0:T(2,128)(2,1)}, u32[]{:S(2)}, u32[]{:S(2)}) collective-permute-start(bf16[1,512,2,256]{3,2,1,0:T(2,128)(2,1)} %bitcast.5), channel_id=1, source_target_pairs={{1,0},{2,1},{3,2},{4,3},{5,4},{6,5},{7,6},{8,7},{9,8},{10,9},{11,1... | collective-permute-start | bytes 1572872 | tf_op jit(solution)/shard_map/ppermute | solution.py:203
  82.6 36.3 %collective-permute-start.3 = (bf16[1,512,2,256]{3,2,1,0:T(2,128)(2,1)}, bf16[1,512,2,256]{3,2,1,0:T(2,128)(2,1)}, u32[]{:S(2)}, u32[]{:S(2)}) collective-permute-start(bf16[1,512,2,256]{3,2,1,0:T(2,128)(2,1)} %bitcast.7), channel_id=1, source_target_pairs={{1,0},{2,1},{3,2},{4,3},{5,4},{6,5},{7,6},{8,7},{9,8},{10,9},{11,1... | collective-permute-start | bytes 1572872 | tf_op jit(solution)/shard_map/ppermute | solution.py:203
  121.0 1.7 copy-start.4
  121.0 1.8 copy-start.3
  122.7 2.2 %copy-start = (bf16[2,2048,512]{2,1,0:T(8,128)(2,1)S(1)}, bf16[2,2048,512]{2,1,0:T(8,128)(2,1)}, u32[]{:S(2)}) copy-start(bf16[2,2048,512]{2,1,0:T(8,128)(2,1)} %h_ref.7) | copy-start | bytes 12582916
  138.8 14.0 %copy-start.2 = (bf16[1,512,512]{2,1,0:T(8,128)(2,1)S(1)}, bf16[1,512,512]{2,1,0:T(8,128)(2,1)}, u32[]{:S(2)}) copy-start(bf16[1,512,512]{2,1,0:T(8,128)(2,1)} %get-tuple-element.7) | copy-start | bytes 1572868
  152.9 14.0 %copy-start.1 = (bf16[1,512,512]{2,1,0:T(8,128)(2,1)S(1)}, bf16[1,512,512]{2,1,0:T(8,128)(2,1)}, u32[]{:S(2)}) copy-start(bf16[1,512,512]{2,1,0:T(8,128)(2,1)} %get-tuple-element.6) | copy-start | bytes 1572868

commit v2 on v1

v2 whole, which is shorter than its diff:
```python
import functools

import jax
import jax.numpy as jnp
from jax import lax
from jax.experimental import pallas as pl
from jax.experimental.pallas import tpu as pltpu
from jax.sharding import PartitionSpec as P

WIN = 9
ROWS = 256
HALO = 128
STRIP = 16
BLOCK = 512
WIDTH = 256


def window_start(tile, size, length):
    return min(max(tile * size - HALO, 0), length - size - 2 * HALO)


def bands(size):
    k = jnp.arange(size + 2 * HALO)[None, :, None]
    n = jnp.arange(size)[None, None, :]
    d = jnp.arange(3)[:, None, None] * HALO
    return (jnp.abs(k - d - n) <= WIN // 2).astype(jnp.bfloat16)


def product_step(step, blocks, x_ref, h_ref, pair_ref, raw_ref, power_ref):
    width = x_ref.shape[2]

    @pl.when(step == 0)
    def _():
        power_ref[...] = jnp.zeros_like(power_ref)
        pair_ref[0, :, :width] = x_ref[0]
        pair_ref[0, :, width:] = x_ref[1]
        pair_ref[1, :, :width] = -x_ref[1]
        pair_ref[1, :, width:] = x_ref[0]

    @pl.when(step < blocks)
    def _():
        rows = pl.ds(pl.multiple_of(step * BLOCK, BLOCK), BLOCK)
        product = jnp.dot(h_ref[0], pair_ref[0], preferred_element_type=jnp.float32)
        product += jnp.dot(h_ref[1], pair_ref[1], preferred_element_type=jnp.float32)
        raw_ref[rows, :] = product
        square = product * product
        square = square[:, :width] + square[:, width:]
        power_ref[...] += jnp.sum(square.reshape(BLOCK // 8, 8, width), axis=0)


def inverse_rms(power_ref, length):
    return lax.rsqrt(jnp.sum(power_ref[...], axis=0, keepdims=True) * (1.0 / length) + 1e-06)


def turned_strip(local, rows, trig_ref, raw_ref, inverse):
    width = inverse.shape[1]
    cosine, sine = trig_ref[local, 0:1], trig_ref[local, 1:2]
    real, imag = raw_ref[rows, :width], raw_ref[rows, width:]
    turned_real = (real * cosine + imag * sine) * inverse
    turned_imag = (imag * cosine - real * sine) * inverse
    return turned_real.astype(jnp.bfloat16), turned_imag.astype(jnp.bfloat16)


def image_kernel(blocks, x_ref, h_ref, trig_ref, image_ref, pair_ref, raw_ref, power_ref):
    step = pl.program_id(1)
    product_step(step, blocks, x_ref, h_ref, pair_ref, raw_ref, power_ref)

    @pl.when(step >= blocks)
    def _():
        base = (step - blocks) * BLOCK
        inverse = inverse_rms(power_ref, blocks * BLOCK)
        for strip in range(BLOCK // STRIP):
            rows = pl.ds(pl.multiple_of(base + strip * STRIP, STRIP), STRIP)
            local = slice(strip * STRIP, (strip + 1) * STRIP)
            real, imag = turned_strip(local, rows, trig_ref, raw_ref, inverse)
            image_ref[0, local, :] = real
            image_ref[1, local, :] = imag


def field_kernel(
    blocks, x_ref, h_ref, trig_ref, own_ref, band_ref, s_ref, pair_ref, raw_ref, power_ref, field_ref
):
    step = pl.program_id(1)
    length = blocks * BLOCK
    product_step(step, blocks, x_ref, h_ref, pair_ref, raw_ref, power_ref)

    @pl.when((step >= blocks) & (step < 2 * blocks))
    def _():
        base = (step - blocks) * BLOCK
        inverse = inverse_rms(power_ref, length)
        for strip in range(BLOCK // STRIP):
            rows = pl.ds(pl.multiple_of(base + strip * STRIP, STRIP), STRIP)
            local = slice(strip * STRIP, (strip + 1) * STRIP)
            other = turned_strip(local, rows, trig_ref, raw_ref, inverse)
            gr, gi = (value.astype(jnp.float32) for value in other)
            fr, fi = (own_ref[k, local, :].astype(jnp.float32) for k in range(2))
            field_ref[0, rows, :] = (fr * gr + fi * gi).astype(jnp.bfloat16)
            field_ref[1, rows, :] = (fi * gr - fr * gi).astype(jnp.bfloat16)
            field_ref[2, rows, :] = (fr * fr + fi * fi).astype(jnp.bfloat16)
            field_ref[3, rows, :] = (gr * gr + gi * gi).astype(jnp.bfloat16)

    @pl.when(step > blocks)
    def _():
        tiles = length // ROWS
        for part in range(BLOCK // ROWS):
            tile = (step - blocks - 1) * (BLOCK // ROWS) + part
            start = jnp.clip(tile * ROWS - HALO, 0, length - ROWS - 2 * HALO)
            rows = pl.ds(pl.multiple_of(start, HALO), ROWS + 2 * HALO)
            which = jnp.where(tile == 0, 0, jnp.where(tile == tiles - 1, 2, 1))
            band = band_ref[which]
            for field in range(4):
                total = jnp.dot(band, field_ref[field, rows, :], preferred_element_type=jnp.float32)
                s_ref[field, part * ROWS : (part + 1) * ROWS, :] = total.astype(jnp.bfloat16)


def focus(pings, matrix, trig, own=None):
    _, depth, ranges = pings.shape
    length = matrix.shape[1]
    blocks = length // BLOCK
    late = 0 if own is None else 1
    planes = 2 if own is None else 4
    in_specs = [
        pl.BlockSpec((2, depth, WIDTH), lambda j, t: (0, 0, j)),
        pl.BlockSpec((2, BLOCK, depth), lambda j, t: (0, jnp.minimum(t, blocks - 1), 0)),
        pl.BlockSpec((BLOCK, 2), lambda j, t: (jnp.clip(t - blocks, 0, blocks - 1), 0)),
    ]
    scratch = [
        pltpu.VMEM((2, depth, 2 * WIDTH), jnp.bfloat16),
        pltpu.VMEM((length, 2 * WIDTH), jnp.float32),
        pltpu.VMEM((8, WIDTH), jnp.float32),
    ]
    operands = [pings, matrix, trig]
    if own is not None:
        band = jnp.swapaxes(bands(ROWS), 1, 2)
        operands += [own, band]
        in_specs += [
            pl.BlockSpec((2, BLOCK, WIDTH), lambda j, t: (0, jnp.clip(t - blocks, 0, blocks - 1), j)),
            pl.BlockSpec(band.shape, lambda j, t: (0, 0, 0)),
        ]
        scratch.append(pltpu.VMEM((4, length, WIDTH), jnp.bfloat16))
    return pl.pallas_call(
        functools.partial(image_kernel if own is None else field_kernel, blocks),
        grid=(ranges // WIDTH, 2 * blocks + late),
        in_specs=in_specs,
        out_specs=pl.BlockSpec(
            (planes, BLOCK, WIDTH), lambda j, t: (0, jnp.clip(t - blocks - late, 0, blocks - 1), j)
        ),
        out_shape=jax.ShapeDtypeStruct((planes, length, ranges), jnp.bfloat16),
        scratch_shapes=scratch,
        compiler_params=pltpu.CompilerParams(
            dimension_semantics=("arbitrary", "arbitrary"), vmem_limit_bytes=20 * 2**20
        ),
        cost_estimate=pl.CostEstimate(
            flops=8 * length * depth * ranges + late * 16 * length * ranges * ROWS,
            bytes_accessed=4 * length * depth + 2 * planes * length * ranges,
            transcendentals=0,
        ),
        name="focus_next" if late else "focus_own",
    )(*operands)


def compare_kernel(band_ref, s_ref, coherence_ref, inter_ref):
    ranges = s_ref.shape[2]
    for part in range(ranges // WIDTH):
        first = window_start(part, WIDTH, ranges)
        band = band_ref[(part * WIDTH - first) // HALO]
        real, imag, own, other = (
            jnp.dot(
                s_ref[field, :, first : first + WIDTH + 2 * HALO], band, preferred_element_type=jnp.float32
            )
            for field in range(4)
        )
        lanes = slice(part * WIDTH, (part + 1) * WIDTH)
        magnitude = jnp.sqrt(real * real + imag * imag)
        coherence_ref[0, :, lanes] = magnitude * lax.rsqrt(own * other + 1e-06)
        inter_ref[0, 0, :, lanes] = (real * (1.0 / (WIN * WIN))).astype(jnp.bfloat16)
        inter_ref[0, 1, :, lanes] = (imag * (1.0 / (WIN * WIN))).astype(jnp.bfloat16)


def compare(sums):
    _, length, ranges = sums.shape
    band = bands(WIDTH)
    return pl.pallas_call(
        compare_kernel,
        grid=(length // ROWS,),
        in_specs=[
            pl.BlockSpec(band.shape, lambda t: (0, 0, 0)),
            pl.BlockSpec((4, ROWS, ranges), lambda t: (0, t, 0)),
        ],
        out_specs=[
            pl.BlockSpec((1, ROWS, ranges), lambda t: (0, t, 0)),
            pl.BlockSpec((1, 2, ROWS, ranges), lambda t: (0, 0, t, 0)),
        ],
        out_shape=[
            jax.ShapeDtypeStruct((1, length, ranges), jnp.float32),
            jax.ShapeDtypeStruct((1, 2, length, ranges), jnp.bfloat16),
        ],
        compiler_params=pltpu.CompilerParams(
            dimension_semantics=("arbitrary",), vmem_limit_bytes=24 * 2**20
        ),
        cost_estimate=pl.CostEstimate(
            flops=16 * length * ranges * WIDTH, bytes_accessed=16 * length * ranges, transcendentals=0
        ),
        name="compare",
    )(band, sums)


def turn_table(angle, length):
    index = angle * jnp.arange(length, dtype=jnp.int32) % length
    phase = 2.0 * jnp.pi / length * index.astype(jnp.float32)
    return jnp.stack([jnp.cos(phase), jnp.sin(phase)], axis=1)


def body(raw_pings, focus_matrix, start_angle, ping_count):
    sectors = lax.axis_size("sector")
    length, depth = focus_matrix.shape[1:]
    position = lax.axis_index("sector")
    following = lax.rem(position + 1, sectors)
    route = [((i + 1) % sectors, i) for i in range(sectors)]
    ping = jnp.arange(depth, dtype=jnp.int32)[:, None, None]

    def masked(block, sector):
        kept = jnp.where(ping < ping_count[sector], block[0], jnp.zeros_like(block[0]))
        return jnp.swapaxes(kept, 0, 1)

    own = lax.all_to_all(raw_pings, "sector", split_axis=0, concat_axis=1, tiled=True)
    other = lax.ppermute(own, "sector", route)
    image = focus(masked(own, position), focus_matrix, turn_table(start_angle[position], length))
    sums = focus(masked(other, following), focus_matrix, turn_table(start_angle[following], length), image)
    return tuple(compare(sums))


def solution(mesh):
    return jax.shard_map(
        body,
        mesh=mesh,
        in_specs=(P("survey", "sector", None, None), P(), P("survey"), P("survey")),
        out_specs=(P(("survey", "sector"), None, None), P(("survey", "sector"), None, None, None)),
        check_vma=False,
    )
```

time: 195 us -> 141 us (0.72)
  blocking collectives: 40.3 us -> 0 us
  waiting for transfers between devices: 17.5 us -> 36.7 us
  local copies, waits for them, and re-layouts: 22.9 us -> 4.23 us
  starting transfers between devices: 32.8 us -> 17.3 us
  Pallas kernels: 68.5 us -> 72.1 us
    all_to_all x2 -> x0, blocking collectives: 40.3 us -> none  [body(): lax.all_to_all(piece, 'sector', split_axis=0, concat_axis=1, tiled=True)]
    all_to_all x2 -> x1, waiting for transfers between devices: 17.5 us -> 36.7 us  [body(): lax.all_to_all(raw_pings, 'sector', split_axis=0, concat_axis=1, tiled=True)]
    reshape x8 -> x0, local copies, waits for them, and re-layouts: 15.8 us -> none  [masked(): flat = block.reshape(depth, -1)]
    ppermute x4 -> x1, starting transfers between devices: 24.4 us -> 9.74 us  [body(): other = lax.ppermute(own, 'sector', route)]
    slice x1 -> x0, local copies, waits for them, and re-layouts: 4.1 us -> none  [body(): piece = raw_pings[:, :, :, chunk * width:(chunk + 1) * width]]
    pallas_call x5 -> x3, Pallas kernels: 68.5 us -> 72.1 us  [the longest x2 59.3 us: focus(): pl.pallas_call(functools.partial(image_kernel if own is None else field_k...]
    select_n x2 -> x1, other arithmetic: 4.53 us -> 1.95 us  [masked(): jnp.where(ping < ping_count[sector], block[0], jnp.zeros_like(block[0]))]
    all_to_all x0 -> x1, local copies, waits for them, and re-layouts: none -> 1.97 us  [body(): lax.all_to_all(raw_pings, 'sector', split_axis=0, concat_axis=1, tiled=True)]
  transfers between devices with their start and end apart: 6 -> 2, of which waited for: 2 -> 1; matrix products, arithmetic and copies ran while one was open for 12% -> 7% of each run, Pallas kernels for 0% -> 14%
where the time goes in v2:
time: 141 us
  Pallas kernels  72.1 us (51%)
  waiting for transfers between devices  36.7 us (26%)
  starting transfers between devices  17.3 us (12%)
  other arithmetic  9.64 us (7%)
  local copies, waits for them, and re-layouts  4.23 us (3%)
    pallas_call x2, Pallas kernels, focus(): pl.pallas_call(functools.partial(image_kernel if own is None else field_k...  59.3 us
    all_to_all x1, waiting for transfers between devices, body(): lax.all_to_all(raw_pings, 'sector', split_axis=0, concat_axis=1, tiled=True)  36.7 us
    pallas_call x1, Pallas kernels, compare(): pl.pallas_call(compare_kernel, grid=(length // ROWS,), in_specs=[pl.Block...  12.8 us
    ppermute x1, starting transfers between devices, body(): other = lax.ppermute(own, 'sector', route)  9.74 us
    all_to_all x1, starting transfers between devices, body(): lax.all_to_all(raw_pings, 'sector', split_axis=0, concat_axis=1, tiled=True)  7.53 us
  transfers between devices with their start and end apart: 2, of which 1 were waited for; matrix products, arithmetic and copies ran while one was open for 7% of the time, Pallas kernels for 14%

profile of v2, /device:TPU:0, one launch (start us, length us, event | category | flops | bytes accessed | tf_op | source)
XLA Modules:
  0.0 140.7 jit_solution(9422721522432989633)
XLA Ops:
  0.6 0.0 copy-start.2
  0.6 0.0 copy-start.1
  0.6 7.5 %all-to-all-start = ((bf16[16,32,2,1024]{3,2,1,0:T(2,128)(2,1)}), bf16[16,32,2,1024]{3,2,1,0:T(2,128)(2,1)S(1)}, u32[]{:S(2)}, u32[]{:S(2)}) async-start(bf16[16,32,2,1024]{3,2,1,0:T(2,128)(2,1)} %param.4), calls=%async_computation | async-start | bytes 4194304 | tf_op jit(solution)/shard_map/all_to_all | solution.py:226
  8.2 0.0 copy-done.2
  8.2 0.0 copy-done.1
  8.2 0.7 fusion.13
  8.9 0.9 fusion.9
  9.8 0.9 fusion.10
  10.7 0.9 fusion.11
  11.6 0.9 fusion.12
  12.6 36.7 %all-to-all-done = bf16[16,32,2,1024]{3,2,1,0:T(2,128)(2,1)S(1)} async-done(((bf16[16,32,2,1024]{3,2,1,0:T(2,128)(2,1)}), bf16[16,32,2,1024]{3,2,1,0:T(2,128)(2,1)S(1)}, u32[]{:S(2)}, u32[]{:S(2)}) %all-to-all-start) | async-done | bytes 2097184 | tf_op jit(solution)/shard_map/all_to_all | solution.py:226
  49.3 2.0 %copy.8 = bf16[16,32,2,1024]{3,1,0,2:T(8,128)(2,1)} copy(bf16[16,32,2,1024]{3,2,1,0:T(2,128)(2,1)S(1)} %all-to-all-done) | data formatting | bytes 4194304 | tf_op jit(solution)/shard_map/all_to_all | solution.py:226
  51.3 9.7 %collective-permute-start = (bf16[1,512,2,1024]{3,1,2,0:T(8,128)(2,1)}, bf16[1,512,2,1024]{3,1,2,0:T(8,128)(2,1)}, u32[]{:S(2)}, u32[]{:S(2)}) collective-permute-start(bf16[1,512,2,1024]{3,1,2,0:T(8,128)(2,1)} %bitcast.1), channel_id=1, source_target_pairs={{1,0},{2,1},{3,2},{4,3},{5,4},{6,5},{7,6},{8,7},{9,8},{10,9},{11,1... | collective-permute-start | bytes 6291464 | tf_op jit(solution)/shard_map/ppermute | solution.py:227
  61.0 0.4 copy.11.trig_ref
  61.4 0.4 copy.10.trig_ref
  61.8 0.7 iota_compare_fusion.1
  62.5 0.7 iota_compare_fusion
  63.1 0.1 iota_subtract_fusion
  63.2 0.4 fusion.2.band_ref
  63.6 0.4 fusion.1.band_ref
  64.0 0.0 copy-start
  64.0 1.9 %bitcast_select_fusion = bf16[512,2,1024]{2,0,1:T(8,128)(2,1)S(1)} fusion(bf16[16,32,2,1024]{3,1,0,2:T(8,128)(2,1)} %copy.8, pred[512]{0:T(512)(128)(4,1)S(1)} %iota_compare_fusion), kind=kLoop, calls=%fused_computation | loop fusion | flops 1048576 | bytes 4194816 | tf_op jit(solution)/shard_map/jit(_where)/select_n | solution.py:223
  66.0 0.9 copy-done
  66.8 20.1 %focus_own.1.own_ref = bf16[2,2048,1024]{2,1,0:T(8,128)(2,1)S(1)} custom-call(bf16[2,512,1024]{2,1,0:T(8,128)(2,1)S(1)} %bitcast.14, bf16[2,2048,512]{2,1,0:T(8,128)(2,1)S(1)} %copy-done, f32[2048,2]{1,0:T(8,128)S(1)} %copy.10.trig_ref), custom_call_target="tpu_custom_call" | custom-call | flops 8589934592 | bytes 12582912 | tf_op jit(solution)/shard_map/focus_own/pallas_call | solution.py:141
  87.0 0.0 collective-permute-done
  87.0 1.8 %fusion.x_ref = bf16[2,512,1024]{2,1,0:T(8,128)(2,1)S(1)} fusion(bf16[1,512,2,1024]{3,1,2,0:T(8,128)(2,1)} %collective-permute-done, pred[512]{0:T(512)(128)(4,1)S(1)} %iota_compare_fusion.1), kind=kLoop, calls=%fused_computation.2 | loop fusion | flops 1048576 | bytes 4194816 | tf_op jit(solution)/shard_map/transpose | solution.py:224
  88.8 39.1 %focus_next.1.s_ref = bf16[4,2048,1024]{2,1,0:T(8,128)(2,1)S(1)} custom-call(bf16[2,512,1024]{2,1,0:T(8,128)(2,1)S(1)} %fusion.x_ref, bf16[2,2048,512]{2,1,0:T(8,128)(2,1)S(1)} %copy-done, f32[2048,2]{1,0:T(8,128)S(1)} %copy.11.trig_ref, bf16[2,2048,1024]{2,1,0:T(8,128)(2,1)S(1)} %focus_own.1.own_ref, bf16[3,256,512]{2,1,0:T(8,128)(2,1)S(1)} %fusion.2.band_ref), custom_call_target="tpu_custom_call" | custom-call | flops 17179869184 | bytes 20971520 | tf_op jit(solution)/shard_map/focus_next/pallas_call | solution.py:141
  127.9 12.8 %compare.22 = (f32[1,2048,1024]{2,1,0:T(8,128)}, bf16[1,2,2048,1024]{3,2,1,0:T(8,128)(2,1)}) custom-call(bf16[3,512,256]{2,1,0:T(8,128)(2,1)S(1)} %fusion.1.band_ref, bf16[4,2048,1024]{2,1,0:T(8,128)(2,1)S(1)} %focus_next.1.s_ref), custom_call_target="tpu_custom_call" | custom-call | flops 8589934592 | bytes 33554432 | tf_op jit(solution)/shard_map/compare/pallas_call | solution.py:183
  (3 shorter events, 0.0 us)
Async XLA Ops:
  0.6 7.6 %copy-start.2 = (s32[16]{0:T(128)S(1)}, s32[16]{0:T(128)}, u32[]{:S(2)}) copy-start(s32[16]{0:T(128)} %param.7) | copy-start | bytes 196
  0.6 7.6 %copy-start.1 = (s32[16]{0:T(128)S(1)}, s32[16]{0:T(128)}, u32[]{:S(2)}) copy-start(s32[16]{0:T(128)} %param.6) | copy-start | bytes 196
  0.6 48.6 %all-to-all-start = ((bf16[16,32,2,1024]{3,2,1,0:T(2,128)(2,1)}), bf16[16,32,2,1024]{3,2,1,0:T(2,128)(2,1)S(1)}, u32[]{:S(2)}, u32[]{:S(2)}) async-start(bf16[16,32,2,1024]{3,2,1,0:T(2,128)(2,1)} %param.4), calls=%async_computation | async-start | bytes 4194304 | tf_op jit(solution)/shard_map/all_to_all | solution.py:226
  51.3 35.7 %collective-permute-start = (bf16[1,512,2,1024]{3,1,2,0:T(8,128)(2,1)}, bf16[1,512,2,1024]{3,1,2,0:T(8,128)(2,1)}, u32[]{:S(2)}, u32[]{:S(2)}) collective-permute-start(bf16[1,512,2,1024]{3,1,2,0:T(8,128)(2,1)} %bitcast.1), channel_id=1, source_target_pairs={{1,0},{2,1},{3,2},{4,3},{5,4},{6,5},{7,6},{8,7},{9,8},{10,9},{11,1... | collective-permute-start | bytes 6291464 | tf_op jit(solution)/shard_map/ppermute | solution.py:227
  64.0 2.8 %copy-start = (bf16[2,2048,512]{2,1,0:T(8,128)(2,1)S(1)}, bf16[2,2048,512]{2,1,0:T(8,128)(2,1)}, u32[]{:S(2)}) copy-start(bf16[2,2048,512]{2,1,0:T(8,128)(2,1)} %h_ref.3) | copy-start | bytes 12582916

commit v3 on v2

--- a/solution.py
+++ b/solution.py
@@ -13,6 +13,7 @@
 STRIP = 16
 BLOCK = 512
 WIDTH = 256
+HALVES = 2
 
 
 def window_start(tile, size, length):
@@ -159,14 +160,26 @@
     )(*operands)
 
 
-def compare_kernel(band_ref, s_ref, coherence_ref, inter_ref):
-    ranges = s_ref.shape[2]
+def lane_window(s_refs, field, first, size):
+    width = s_refs[0].shape[2]
+    pieces = []
+    for index, s_ref in enumerate(s_refs):
+        low = max(first - index * width, 0)
+        high = min(first + size - index * width, width)
+        if high > low:
+            pieces.append(s_ref[field, :, low:high])
+    return jnp.concatenate(pieces, axis=1) if len(pieces) > 1 else pieces[0]
+
+
+def compare_kernel(band_ref, *refs):
+    s_refs, (coherence_ref, inter_ref) = refs[:HALVES], refs[HALVES:]
+    ranges = s_refs[0].shape[2] * HALVES
     for part in range(ranges // WIDTH):
         first = window_start(part, WIDTH, ranges)
         band = band_ref[(part * WIDTH - first) // HALO]
         real, imag, own, other = (
             jnp.dot(
-                s_ref[field, :, first : first + WIDTH + 2 * HALO], band, preferred_element_type=jnp.float32
+                lane_window(s_refs, field, first, WIDTH + 2 * HALO), band, preferred_element_type=jnp.float32
             )
             for field in range(4)
         )
@@ -178,15 +191,16 @@
 
 
 def compare(sums):
-    _, length, ranges = sums.shape
+    _, length, width = sums[0].shape
+    ranges = width * HALVES
     band = bands(WIDTH)
     return pl.pallas_call(
         compare_kernel,
         grid=(length // ROWS,),
         in_specs=[
             pl.BlockSpec(band.shape, lambda t: (0, 0, 0)),
-            pl.BlockSpec((4, ROWS, ranges), lambda t: (0, t, 0)),
-        ],
+        ]
+        + [pl.BlockSpec((4, ROWS, width), lambda t: (0, t, 0))] * HALVES,
         out_specs=[
             pl.BlockSpec((1, ROWS, ranges), lambda t: (0, t, 0)),
             pl.BlockSpec((1, 2, ROWS, ranges), lambda t: (0, 0, t, 0)),
@@ -202,7 +216,7 @@
             flops=16 * length * ranges * WIDTH, bytes_accessed=16 * length * ranges, transcendentals=0
         ),
         name="compare",
-    )(band, sums)
+    )(band, *sums)
 
 
 def turn_table(angle, length):
@@ -223,10 +237,21 @@
         kept = jnp.where(ping < ping_count[sector], block[0], jnp.zeros_like(block[0]))
         return jnp.swapaxes(kept, 0, 1)
 
-    own = lax.all_to_all(raw_pings, "sector", split_axis=0, concat_axis=1, tiled=True)
-    other = lax.ppermute(own, "sector", route)
-    image = focus(masked(own, position), focus_matrix, turn_table(start_angle[position], length))
-    sums = focus(masked(other, following), focus_matrix, turn_table(start_angle[following], length), image)
+    width = raw_pings.shape[3] // HALVES
+    tables = [turn_table(start_angle[sector], length) for sector in (position, following)]
+    received = []
+    for half in range(HALVES):
+        piece = raw_pings[:, :, :, half * width : (half + 1) * width]
+        if received:
+            piece, received[-1] = lax.optimization_barrier((piece, received[-1]))
+        received.append(lax.all_to_all(piece, "sector", split_axis=0, concat_axis=1, tiled=True))
+    sums = []
+    for own in received:
+        if sums:
+            own, sums[-1] = lax.optimization_barrier((own, sums[-1]))
+        other = lax.ppermute(own, "sector", route)
+        image = focus(masked(own, position), focus_matrix, tables[0])
+        sums.append(focus(masked(other, following), focus_matrix, tables[1], image))
     return tuple(compare(sums))
 
 

time: 141 us -> 140 us (level)
  the two profiles are of different devices: /device:TPU:0 before, /device:TPU:13 now
where the time goes in v3:
time: 140 us; the launch traced here: 139 us
  Pallas kernels  70 us (50%)
  waiting for transfers between devices  31.5 us (22%)
  starting transfers between devices  14.4 us (10%)
  local copies, waits for them, and re-layouts  13.8 us (10%)
  other arithmetic  8.67 us (6%)
    pallas_call x4, Pallas kernels, focus(): pl.pallas_call(functools.partial(image_kernel if own is None else field_k...  57.2 us
    all_to_all x2, waiting for transfers between devices, body(): lax.all_to_all(piece, 'sector', split_axis=0, concat_axis=1, tiled=True)  20.6 us
    all_to_all x2, starting transfers between devices, body(): lax.all_to_all(piece, 'sector', split_axis=0, concat_axis=1, tiled=True)  14.1 us
    pallas_call x1, Pallas kernels, compare(): pl.pallas_call(compare_kernel, grid=(length // ROWS,), in_specs=[pl.Block...  12.8 us
    ppermute x2, waiting for transfers between devices, body(): other = lax.ppermute(own, 'sector', route)  10.9 us
    unnamed x16, local copies, waits for them, and re-layouts  5.88 us
    slice x1, local copies, waits for them, and re-layouts, body(): piece = raw_pings[:, :, :, half * width:(half + 1) * width]  3.73 us
    transpose x4, other arithmetic, masked(): return jnp.swapaxes(kept, 0, 1)  3.01 us
  transfers between devices with their start and end apart: 4, of which 3 were waited for; matrix products, arithmetic and copies ran while one was open for 7% of the time, Pallas kernels for 28%

profile of v3, /device:TPU:13, one launch (start us, length us, event | category | flops | bytes accessed | tf_op | source)
XLA Modules:
  0.0 139.2 jit_solution(2876291121842468270)
XLA Ops:
  0.6 3.7 %fusion.16 = (bf16[16,32,2,512]{3,2,1,0:T(2,128)(2,1)}, bf16[16,32,2,512]{3,2,1,0:T(2,128)(2,1)}) fusion(bf16[16,32,2,1024]{3,2,1,0:T(2,128)(2,1)} %param.4), kind=kLoop, calls=%fused_computation.34 | loop fusion | bytes 4194304 | tf_op jit(solution)/shard_map/slice | solution.py:244
  4.4 0.0 copy-start.4
  4.4 0.0 copy-start.5
  4.4 6.7 %all-to-all-start = ((bf16[16,32,2,512]{3,2,1,0:T(2,128)(2,1)}), bf16[16,32,2,512]{3,2,1,0:T(2,128)(2,1)S(1)}, u32[]{:S(2)}, u32[]{:S(2)}) async-start(bf16[16,32,2,512]{3,2,1,0:T(2,128)(2,1)} %get-tuple-element.10), calls=%async_computation | async-start | bytes 2097152 | tf_op jit(solution)/shard_map/all_to_all | solution.py:247
  11.1 0.0 copy-done.4
  11.1 0.0 copy-done.5
  11.1 0.7 fusion.17
  11.8 0.8 fusion.12
  12.6 0.8 fusion.13
  13.4 0.9 fusion.14
  14.3 0.9 fusion.15
  15.3 0.1 iota_subtract_fusion
  15.4 20.6 %all-to-all-done = bf16[16,32,2,512]{3,2,1,0:T(2,128)(2,1)S(1)} async-done(((bf16[16,32,2,512]{3,2,1,0:T(2,128)(2,1)}), bf16[16,32,2,512]{3,2,1,0:T(2,128)(2,1)S(1)}, u32[]{:S(2)}, u32[]{:S(2)}) %all-to-all-start) | async-done | bytes 1048608 | tf_op jit(solution)/shard_map/all_to_all | solution.py:247
  35.9 1.2 copy.8
  37.1 0.2 collective-permute-start
  37.3 0.7 iota_compare_fusion.1
  38.0 0.4 copy.11.trig_ref
  38.4 0.4 copy.10.trig_ref
  38.8 0.6 iota_compare_fusion
  39.4 7.4 %all-to-all-start.1 = ((bf16[16,32,2,512]{3,2,1,0:T(2,128)(2,1)}), bf16[16,32,2,512]{3,2,1,0:T(2,128)(2,1)}, u32[]{:S(2)}, u32[]{:S(2)}) async-start(bf16[16,32,2,512]{3,2,1,0:T(2,128)(2,1)} %get-tuple-element.6), calls=%async_computation.1 | async-start | bytes 2097152 | tf_op jit(solution)/shard_map/all_to_all | solution.py:247
  46.8 0.4 fusion.1.band_ref
  47.2 1.4 fusion.4.x_ref
  48.6 0.0 copy-start
  48.6 2.2 %copy-done = bf16[2,2048,512]{2,1,0:T(8,128)(2,1)S(1)} copy-done((bf16[2,2048,512]{2,1,0:T(8,128)(2,1)S(1)}, bf16[2,2048,512]{2,1,0:T(8,128)(2,1)}, u32[]{:S(2)}) %copy-start) | copy-done | bytes 4194328
  50.8 0.0 copy-start.1
  50.8 9.8 %focus_own.2.own_ref = bf16[2,2048,512]{2,1,0:T(8,128)(2,1)S(1)} custom-call(bf16[2,512,512]{2,1,0:T(8,128)(2,1)S(1)} %fusion.4.x_ref, bf16[2,2048,512]{2,1,0:T(8,128)(2,1)S(1)} %copy-done, f32[2048,2]{1,0:T(8,128)S(1)} %copy.10.trig_ref), custom_call_target="tpu_custom_call" | custom-call | flops 4294967296 | bytes 8388608 | tf_op jit(solution)/shard_map/focus_own/pallas_call | solution.py:142
  60.6 6.5 %collective-permute-done = bf16[1,512,2,512]{3,1,2,0:T(8,128)(2,1)} collective-permute-done((bf16[1,512,2,512]{3,1,2,0:T(8,128)(2,1)}, bf16[1,512,2,512]{3,1,2,0:T(8,128)(2,1)}, u32[]{:S(2)}, u32[]{:S(2)}) %collective-permute-start) | collective-permute-done | bytes 1048608 | tf_op jit(solution)/shard_map/ppermute | solution.py:252
  67.1 1.4 fusion.5.x_ref
  68.4 0.0 copy-done.1
  68.5 18.8 %focus_next.2.refs_0_ = bf16[4,2048,512]{2,1,0:T(8,128)(2,1)S(1)} custom-call(bf16[2,512,512]{2,1,0:T(8,128)(2,1)S(1)} %fusion.5.x_ref, bf16[2,2048,512]{2,1,0:T(8,128)(2,1)S(1)} %copy-done.1, f32[2048,2]{1,0:T(8,128)S(1)} %copy.11.trig_ref, bf16[2,2048,512]{2,1,0:T(8,128)(2,1)S(1)} %focus_own.2.own_ref, bf16[3,256,512]{2,1,0:T(8,128)(2,1)S(1)} %fusion.1.band_ref), custom_call_target="tpu_custom_call" | custom-call | flops 8589934592 | bytes 12582912 | tf_op jit(solution)/shard_map/focus_next/pallas_call | solution.py:142
  87.3 0.0 copy-start.3
  87.3 3.4 %copy-done.3 = bf16[4,2048,512]{2,1,0:T(8,128)(2,1)} copy-done((bf16[4,2048,512]{2,1,0:T(8,128)(2,1)}, bf16[4,2048,512]{2,1,0:T(8,128)(2,1)S(1)}, u32[]{:S(2)}) %copy-start.3) | copy-done | bytes 8388632
  90.7 0.0 all-to-all-done.1
  90.7 0.0 copy-start.2
  90.7 1.6 %copy.9 = bf16[16,32,2,512]{3,1,0,2:T(8,128)(2,1)S(1)} copy(bf16[16,32,2,512]{3,2,1,0:T(2,128)(2,1)} %all-to-all-done.1) | data formatting | bytes 2097152 | tf_op jit(solution)/shard_map/all_to_all | solution.py:247
  92.3 0.1 collective-permute-start.1
  92.4 0.4 fusion.band_ref
  92.8 0.1 fusion.2.x_ref
  92.9 0.3 copy-done.2
  93.2 9.8 %focus_own.3.own_ref = bf16[2,2048,512]{2,1,0:T(8,128)(2,1)S(1)} custom-call(bf16[2,512,512]{2,1,0:T(8,128)(2,1)S(1)} %fusion.2.x_ref, bf16[2,2048,512]{2,1,0:T(8,128)(2,1)S(1)} %copy-done.2, f32[2048,2]{1,0:T(8,128)S(1)} %copy.10.trig_ref), custom_call_target="tpu_custom_call" | custom-call | flops 4294967296 | bytes 8388608 | tf_op jit(solution)/shard_map/focus_own/pallas_call | solution.py:142
  103.0 4.5 %collective-permute-done.1 = bf16[1,512,2,512]{3,1,2,0:T(8,128)(2,1)S(1)} collective-permute-done((bf16[1,512,2,512]{3,1,2,0:T(8,128)(2,1)S(1)}, bf16[1,512,2,512]{3,1,2,0:T(8,128)(2,1)S(1)}, u32[]{:S(2)}, u32[]{:S(2)}) %collective-permute-start.1) | collective-permute-done | bytes 1048608 | tf_op jit(solution)/shard_map/ppermute | solution.py:252
  107.5 0.0 slice-start
  107.5 0.1 fusion.3.x_ref
  107.6 0.0 slice-start.1
  107.6 18.8 %focus_next.3.refs_1_ = bf16[4,2048,512]{2,1,0:T(8,128)(2,1)S(1)} custom-call(bf16[2,512,512]{2,1,0:T(8,128)(2,1)S(1)} %fusion.3.x_ref, bf16[2,2048,512]{2,1,0:T(8,128)(2,1)S(1)} %copy-done.2, f32[2048,2]{1,0:T(8,128)S(1)} %copy.11.trig_ref, bf16[2,2048,512]{2,1,0:T(8,128)(2,1)S(1)} %focus_own.3.own_ref, bf16[3,256,512]{2,1,0:T(8,128)(2,1)S(1)} %fusion.1.band_ref), custom_call_target="tpu_custom_call" | custom-call | flops 8589934592 | bytes 12582912 | tf_op jit(solution)/shard_map/focus_next/pallas_call | solution.py:142
  126.4 0.0 slice-done
  126.5 0.0 slice-done.1
  126.5 12.8 %compare.22 = (f32[1,2048,1024]{2,1,0:T(8,128)}, bf16[1,2,2048,1024]{3,2,1,0:T(8,128)(2,1)}) custom-call(bf16[3,512,256]{2,1,0:T(8,128)(2,1)S(1)} %fusion.band_ref, bf16[4,2048,512]{2,1,0:T(8,128)(2,1)S(1)} %bitcast.31, bf16[4,2048,512]{2,1,0:T(8,128)(2,1)S(1)} %focus_next.3.refs_1_), custom_call_target="tpu_custom_call" | custom-call | flops 8589934592 | bytes 33554432 | tf_op jit(solution)/shard_map/compare/pallas_call | solution.py:197
  (4 shorter events, 0.0 us)
Async XLA Ops:
  4.4 6.7 %copy-start.4 = (s32[16]{0:T(128)S(1)}, s32[16]{0:T(128)}, u32[]{:S(2)}) copy-start(s32[16]{0:T(128)} %param.6) | copy-start | bytes 196
  4.4 6.7 %copy-start.5 = (s32[16]{0:T(128)S(1)}, s32[16]{0:T(128)}, u32[]{:S(2)}) copy-start(s32[16]{0:T(128)} %param.7) | copy-start | bytes 196
  4.4 31.6 %all-to-all-start = ((bf16[16,32,2,512]{3,2,1,0:T(2,128)(2,1)}), bf16[16,32,2,512]{3,2,1,0:T(2,128)(2,1)S(1)}, u32[]{:S(2)}, u32[]{:S(2)}) async-start(bf16[16,32,2,512]{3,2,1,0:T(2,128)(2,1)} %get-tuple-element.10), calls=%async_computation | async-start | bytes 2097152 | tf_op jit(solution)/shard_map/all_to_all | solution.py:247
  37.1 29.9 %collective-permute-start = (bf16[1,512,2,512]{3,1,2,0:T(8,128)(2,1)}, bf16[1,512,2,512]{3,1,2,0:T(8,128)(2,1)}, u32[]{:S(2)}, u32[]{:S(2)}) collective-permute-start(bf16[1,512,2,512]{3,1,2,0:T(8,128)(2,1)} %bitcast), channel_id=1, source_target_pairs={{1,0},{2,1},{3,2},{4,3},{5,4},{6,5},{7,6},{8,7},{9,8},{10,9},{11,1... | collective-permute-start | bytes 3145736 | tf_op jit(solution)/shard_map/ppermute | solution.py:252
  39.4 51.3 %all-to-all-start.1 = ((bf16[16,32,2,512]{3,2,1,0:T(2,128)(2,1)}), bf16[16,32,2,512]{3,2,1,0:T(2,128)(2,1)}, u32[]{:S(2)}, u32[]{:S(2)}) async-start(bf16[16,32,2,512]{3,2,1,0:T(2,128)(2,1)} %get-tuple-element.6), calls=%async_computation.1 | async-start | bytes 2097152 | tf_op jit(solution)/shard_map/all_to_all | solution.py:247
  48.6 2.2 %copy-start = (bf16[2,2048,512]{2,1,0:T(8,128)(2,1)S(1)}, bf16[2,2048,512]{2,1,0:T(8,128)(2,1)}, u32[]{:S(2)}) copy-start(bf16[2,2048,512]{2,1,0:T(8,128)(2,1)} %h_ref.7) | copy-start | bytes 12582916
  50.8 17.7 %copy-start.1 = (bf16[2,2048,512]{2,1,0:T(8,128)(2,1)S(1)}, bf16[2,2048,512]{2,1,0:T(8,128)(2,1)}, u32[]{:S(2)}) copy-start(bf16[2,2048,512]{2,1,0:T(8,128)(2,1)} %h_ref.7) | copy-start | bytes 12582916
  87.3 3.4 %copy-start.3 = (bf16[4,2048,512]{2,1,0:T(8,128)(2,1)}, bf16[4,2048,512]{2,1,0:T(8,128)(2,1)S(1)}, u32[]{:S(2)}) copy-start(bf16[4,2048,512]{2,1,0:T(8,128)(2,1)S(1)} %focus_next.2.refs_0_) | copy-start | bytes 25165828
  90.7 2.5 %copy-start.2 = (bf16[2,2048,512]{2,1,0:T(8,128)(2,1)S(1)}, bf16[2,2048,512]{2,1,0:T(8,128)(2,1)}, u32[]{:S(2)}) copy-start(bf16[2,2048,512]{2,1,0:T(8,128)(2,1)} %h_ref.7) | copy-start | bytes 12582916
  92.3 15.2 %collective-permute-start.1 = (bf16[1,512,2,512]{3,1,2,0:T(8,128)(2,1)S(1)}, bf16[1,512,2,512]{3,1,2,0:T(8,128)(2,1)S(1)}, u32[]{:S(2)}, u32[]{:S(2)}) collective-permute-start(bf16[1,512,2,512]{3,1,2,0:T(8,128)(2,1)S(1)} %bitcast.32), channel_id=1, source_target_pairs={{1,0},{2,1},{3,2},{4,3},{5,4},{6,5},{7,6},{8,7},{9,8},{10,9},{11,1... | collective-permute-start | bytes 3145736 | tf_op jit(solution)/shard_map/ppermute | solution.py:252
  107.5 19.0 %slice-start = ((s8[8388608]{0:T(1024)(128)(4,1)}), s8[4194304]{0:T(1024)(128)(4,1)S(1)}, s32[]{:S(2)}) async-start(s8[8388608]{0:T(1024)(128)(4,1)} %bitcast.30), calls=%async_computation.2 | async-start | bytes 8388608
  107.6 18.8 %slice-start.1 = ((s8[8388608]{0:T(1024)(128)(4,1)}), s8[4194304]{0:T(1024)(128)(4,1)S(1)}, s32[]{:S(2)}) async-start(s8[8388608]{0:T(1024)(128)(4,1)} %bitcast.30), calls=%async_computation.3 | async-start | bytes 8388608
